TPU v7x, 32 devices: a whole 2x2x4 slice. The times are simulated.
32 devices in a mesh: groups: 2 (over y), seq: 4 (over z), mp: 2 (over x), section: 2 (over core).
Axes of the slice: x: 2, y: 2, z: 4, core: 2. Of those that a mesh axis runs over, the one named last changes fastest.
Arguments:
- readout: bfloat16 [8, 64, 32, 1024], P(('groups', 'mp', 'section'), None, 'seq'), parts along dimension 0, may hold values from -6 to 6
- first_kernel: bfloat16 [3, 3, 64, 128], replicated, may hold values from -0.25 to 0.25
- second_kernel: bfloat16 [3, 3, 128, 256], replicated, may hold values from -0.1875 to 0.1875
- embed_weight: bfloat16 [1024, 768], P(('mp', 'section')), may hold values from -0.1875 to 0.1875
- project_weight: bfloat16 [768, 2304], P(('mp', 'section'))
- output_weight: bfloat16 [768, 768], P(('mp', 'section')), may hold values from -0.4375 to 0.4375
- order: int32 [8, 512], P(('groups', 'mp', 'section')), parts along dimension 0, may hold values from 0 to 511, as said below
- active: int32 [8, 512], P(('groups', 'mp', 'section'), 'seq'), parts along dimension 0, may hold values 0 or 1
Outputs:
- encoded: bfloat16 [8, 512, 768], P(('groups', 'mp', 'section'), 'seq'), parts along dimension 0
There are 2 independent parts, one for each index of `groups`. A program takes and returns all parts, laid end to end along the dimension named above; an argument that names none is the same for every part. Nothing has to cross between parts.
Inputs may be any that keep to these rules, and one draw needn't show every extreme that they name: Each row of order lists each of the 512 patches of its region once. Patch i comes from the wire tile i // 128; each block of 128 positions k * 128 to (k + 1) * 128 - 1 holds exactly 32 patches of every wire tile.
All inputs are finite; a program needn't handle non-finite values. No bound on the sum of `active` on one device may be relied on, other than what follows from the above.
Results may differ from a plain program's by a relative error of at most 0.017.
Values may be sent and summed in bfloat16 or wider, within the bound.
A program may use at most 64 MiB of HBM per device.

v0:
```python
import jax
import jax.numpy as jnp
from jax import lax
from jax.sharding import PartitionSpec as P

HEADS = 12


masked_score = -1e30
epsilon = 1e-05


def shifted(value, axis, steps):
    count = lax.axis_size(axis)
    first, last = (max(0, -steps), min(count, count - steps))
    return lax.ppermute(value, axis, [(source, source + steps) for source in range(first, last)])


def strided_conv(padded, kernel):
    result = lax.conv_general_dilated(
        padded[None],
        kernel,
        (2, 2),
        "VALID",
        dimension_numbers=("NCHW", "HWIO", "NCHW"),
        preferred_element_type=jnp.float32,
    )[0]
    return jax.nn.silu(result).astype(jnp.bfloat16)


def extend_low(tile, lower_row):
    joined = jnp.concatenate([lower_row, tile], axis=1)
    return jnp.pad(joined, ((0, 0), (0, 0), (1, 0)))


def normalize(tokens):
    values = tokens.astype(jnp.float32)
    center = jnp.mean(values, axis=-1, keepdims=True)
    spread = jnp.mean(jnp.square(values - center), axis=-1, keepdims=True)
    return ((values - center) * lax.rsqrt(spread + epsilon)).astype(jnp.bfloat16)


def patch_rows(features):
    channels, height, length = features.shape
    grid = features.reshape(channels, height // 2, 2, length // 2, 2)
    return grid.transpose(1, 3, 0, 2, 4).reshape(height // 2 * (length // 2), channels * 4)


def accumulate(carry, query_heads, query_pos, keys_piece, values_piece, flag_piece):
    summed, running, weight_sum = carry
    length = keys_piece.shape[0]
    head_count = query_heads.shape[1]
    head_size = query_heads.shape[2]
    key_heads = keys_piece.reshape(length, head_count, head_size)
    value_heads = values_piece.reshape(length, head_count, head_size)
    scores = jnp.einsum("qhd,khd->qhk", query_heads, key_heads, preferred_element_type=jnp.float32)
    key_pos = jnp.arange(length, dtype=jnp.int32)
    allowed = ((flag_piece[None, :] > 0.5) | (key_pos[None, :] == query_pos[:, None]))[:, None, :]
    scores = jnp.where(allowed, scores, masked_score)
    updated = jnp.maximum(running, jnp.max(scores, axis=-1))
    weights = jnp.where(allowed, jnp.exp(scores - updated[..., None]), 0.0)
    factor = jnp.exp(running - updated)
    added = jnp.einsum(
        "qhk,khd->qhd",
        weights.astype(jnp.bfloat16),
        value_heads,
        preferred_element_type=jnp.float32,
    )
    return (
        summed * factor[..., None] + added,
        updated,
        weight_sum * factor + jnp.sum(weights, axis=-1),
    )


def empty_state(rows, head_count, head_size):
    return (
        jnp.zeros((rows, head_count, head_size), jnp.float32),
        jnp.full((rows, head_count), masked_score, jnp.float32),
        jnp.zeros((rows, head_count), jnp.float32),
    )


def body(
    readout, first_kernel, second_kernel, embed_weight, project_weight, output_weight, order, active
):
    shards = lax.axis_size("seq")
    position = lax.axis_index("seq")
    embed_full, project_full, output_full = (
        lax.all_gather(embed_weight, ("mp", "section"), axis=0, tiled=True),
        lax.all_gather(project_weight, ("mp", "section"), axis=0, tiled=True),
        lax.all_gather(output_weight, ("mp", "section"), axis=0, tiled=True),
    )
    level_zero = readout[0]
    lower_first = shifted(level_zero[:, -1:, :], "seq", 1)
    level_one = strided_conv(extend_low(level_zero, lower_first), first_kernel)
    lower_second = shifted(level_one[:, -1:, :], "seq", 1)
    level_two = strided_conv(extend_low(level_one, lower_second), second_kernel)
    patches = patch_rows(level_two)
    count = patches.shape[0]
    group = count // shards
    width = embed_full.shape[1]
    sequence = order[0]
    blocks = sequence.reshape(shards, count)
    columns = jnp.arange(count, dtype=jnp.int32)
    ranked = jnp.where(blocks // count == position, count - columns[None, :], 0)
    picked = lax.top_k(ranked, group)[1]
    outgoing_rows = (jnp.take_along_axis(blocks, picked, axis=1) % count).reshape(-1)
    own_block = lax.dynamic_slice_in_dim(sequence, position * count, count)
    source = own_block // count
    member = (source[:, None] == jnp.arange(shards, dtype=jnp.int32)[None, :]).astype(jnp.int32)
    earlier = jnp.sum((jnp.cumsum(member, axis=0) - member) * member, axis=1)
    arrival = source * group + earlier
    outgoing = patches[outgoing_rows].reshape(shards, group, patches.shape[1])
    received = lax.all_to_all(outgoing, "seq", split_axis=0, concat_axis=0, tiled=True)
    placed = received.reshape(count, patches.shape[1])[arrival]
    tokens = jnp.dot(placed, embed_full, preferred_element_type=jnp.float32).astype(jnp.bfloat16)
    normed = normalize(tokens)
    head_size = width // HEADS
    projected = jnp.dot(normed, project_full, preferred_element_type=jnp.float32)
    query_flat = (projected[:, :width] * head_size ** (-0.5)).astype(jnp.bfloat16)
    queries = query_flat.reshape(count, HEADS, head_size)
    query_pos = position * count + columns
    flags = active[0].astype(jnp.bfloat16)
    initial = empty_state(count, HEADS, head_size)
    keys_flat = projected[:, width : 2 * width].astype(jnp.bfloat16)
    values_flat = projected[:, 2 * width :].astype(jnp.bfloat16)
    summed, running, weight_sum = accumulate(
        initial,
        queries,
        query_pos,
        lax.all_gather(keys_flat, "seq", axis=0, tiled=True),
        lax.all_gather(values_flat, "seq", axis=0, tiled=True),
        lax.all_gather(flags, "seq", axis=0, tiled=True),
    )
    mixed = (summed / weight_sum[..., None]).astype(jnp.bfloat16).reshape(count, width)
    result = tokens.astype(jnp.float32) + jnp.dot(
        mixed, output_full, preferred_element_type=jnp.float32
    )
    return result.astype(jnp.bfloat16)[None]


def solution(mesh):
    in_specs = (
        P(("groups", "mp", "section"), None, "seq", None),
        P(),
        P(),
        P(("mp", "section"), None),
        P(("mp", "section"), None),
        P(("mp", "section"), None),
        P(("groups", "mp", "section"), None),
        P(("groups", "mp", "section"), "seq"),
    )
    out_specs = P(("groups", "mp", "section"), "seq", None)
    return jax.shard_map(body, mesh=mesh, in_specs=in_specs, out_specs=out_specs, check_vma=False)
```

profile of v0, /device:TPU:0, one launch (start us, length us, event | category | flops | bytes accessed | tf_op | source)
XLA Modules:
  0.0 125.2 jit_solution(1145322353449359863)
XLA Ops:
  7.4 1.4 %fusion.63 = s32[4,128]{1,0:T(4,128)} fusion(s32[4,128]{1,0:T(4,128)} %bitcast.108, s32[128]{0:T(128)S(1)} %iota_subtract_fusion, s32[]{:T(128)S(6)} %axis_index.15), kind=kLoop, calls=%fused_computation.91 | loop fusion | flops 8704 | bytes 4612 | tf_op jit(solution)/shard_map/jit(_where)/select_n | solution.py:106
  8.8 0.6 top_k.10
  10.0 0.5 all-gather.7.cloned.1.call-update
  10.6 1.5 %slice.34 = bf16[64,1,1024]{2,1,0:T(2,128)(2,1)S(1)} slice(bf16[64,8,1024]{2,1,0:T(8,128)(2,1)} %bitcast.116), slice={[0:64], [7:8], [0:1024]} | slice | bytes 262144 | tf_op jit(solution)/shard_map/slice | solution.py:95
  12.1 4.9 %collective-permute-start = (bf16[64,1,1024]{2,1,0:T(2,128)(2,1)S(1)}, bf16[64,1,1024]{2,1,0:T(2,128)(2,1)S(1)}, u32[]{:S(2)}, u32[]{:S(2)}) collective-permute-start(bf16[64,1,1024]{2,1,0:T(2,128)(2,1)S(1)} %slice.34), channel_id=1, source_target_pairs={{0,4},{4,8},{8,12},{1,5},{5,9},{9,13},{2,6},{6,10},{10,14},{3,7},{... | collective-permute-start | bytes 393224 | tf_op jit(solution)/shard_map/ppermute | solution.py:16
  17.1 0.7 and_select_fusion
  18.3 0.7 bitcast_or_fusion
  19.1 1.5 %gather_fusion.2 = s32[128]{0:T(128)S(1)} fusion(s32[4,128]{1,0:T(4,128)S(1)} %bitcast.109, s32[128]{0:T(128)S(1)} %reshape.338), kind=kCustom, calls=%fused_computation.2 | custom fusion | bytes 2048 | tf_op jit(solution)/shard_map/jit(take_along_axis)/gather | solution.py:108
  20.7 0.7 and_select_fusion.3
  21.4 1.2 collective-permute-done
  22.6 2.4 %fusion.14 = bf16[64,9,1,1025]{3,1,0,2:T(8,128)(2,1)S(1)} fusion(bf16[64,8,1024]{2,1,0:T(8,128)(2,1)S(1)} %bitcast.117, bf16[64,1,1024]{2,1,0:T(2,128)(2,1)S(1)} %collective-permute-done), kind=kLoop, calls=%fused_computation.20 | loop fusion | flops 4132800 | bytes 2360448 | tf_op jit(solution)/shard_map/broadcast_in_dim | solution.py:21
  25.3 4.4 %reshape.352 = bf16[64,9,1,8,130]{4,3,1,0,2:T(8,128)(2,1)} reshape(bf16[64,9,1,1040]{3,1,0,2:T(8,128)(2,1)S(1)} %pad.10) | data formatting | bytes 2396160 | tf_op jit(solution)/shard_map/conv_general_dilated | solution.py:20
  29.7 6.0 %copy.29 = bf16[64,9,1,8,130]{0,3,4,1,2:T(8,128)(2,1)S(1)} copy(bf16[64,9,1,8,130]{4,3,1,0,2:T(8,128)(2,1)} %reshape.352) | data formatting | bytes 2396160 | tf_op jit(solution)/shard_map/conv_general_dilated | solution.py:20
  35.8 1.1 fusion.24
  37.1 0.6 fusion.39
  38.0 4.4 %collective-permute-start.1 = (bf16[128,1,512]{0,1,2:T(2,128)(2,1)S(1)}, bf16[128,1,512]{0,1,2:T(2,128)(2,1)S(1)}, u32[]{:S(2)}, u32[]{:S(2)}) collective-permute-start(bf16[128,1,512]{0,1,2:T(2,128)(2,1)S(1)} %slice.37), channel_id=1, source_target_pairs={{0,4},{4,8},{8,12},{1,5},{5,9},{9,13},{2,6},{6,10},{10,14},{3,7},{... | collective-permute-start | bytes 393224 | tf_op jit(solution)/shard_map/ppermute | solution.py:16
  42.4 4.6 %collective-permute-done.1 = bf16[128,1,512]{0,1,2:T(2,128)(2,1)S(1)} collective-permute-done((bf16[128,1,512]{0,1,2:T(2,128)(2,1)S(1)}, bf16[128,1,512]{0,1,2:T(2,128)(2,1)S(1)}, u32[]{:S(2)}, u32[]{:S(2)}) %collective-permute-start.1) | collective-permute-done | bytes 131104 | tf_op jit(solution)/shard_map/ppermute | solution.py:16
  47.0 0.5 fusion.38
  50.1 1.6 %gather_fusion = bf16[128,1024]{1,0:T(8,128)(2,1)} fusion(bf16[128,1024]{1,0:T(8,128)(2,1)S(1)} %copy.38, s32[1024]{0:T(1024)S(1)} %pad_clamp_fusion.1), kind=kCustom, calls=%fused_computation | custom fusion | bytes 524800 | tf_op jit(solution)/shard_map/gather | solution.py:114
  51.7 5.8 %all-to-all-start = ((bf16[4,32,1024]{2,1,0:T(8,128)(2,1)}), bf16[4,32,1024]{2,1,0:T(8,128)(2,1)S(1)}, u32[]{:S(2)}, u32[]{:S(2)}) async-start(bf16[4,32,1024]{2,1,0:T(8,128)(2,1)} %bitcast.19), calls=%async_computation | async-start | bytes 524288 | tf_op jit(solution)/shard_map/all_to_all | solution.py:115
  57.5 11.5 %all-gather = bf16[1,512]{1,0:T(2,128)(2,1)S(1)} all-gather(bf16[1,128]{1,0:T(2,128)(2,1)S(1)} %convert_element_type.55), channel_id=2, replica_groups=mesh['groups'=2,'seq'=4,'mp'=2,'section'=2] {'seq'}, dimensions={1}, use_global_device_ids=true | all-gather | bytes 1280 | tf_op jit(solution)/shard_map/all_gather | solution.py:134
  69.0 0.8 fusion.55
  69.8 0.9 gather_fusion.1
  70.7 1.9 %fusion.77 = (f32[128]{0:T(128)S(1)}, f32[128,768]{1,0:T(8,128)S(1)}) fusion(bf16[128,1024]{1,0:T(8,128)(2,1)S(1)} %gather_fusion.1, bf16[1024,768]{1,0:T(8,128)(2,1)} %all-gather.5.cloned.1.call-done), kind=kOutput, calls=%fused_computation.119 | convolution fusion | flops 201621376 | bytes 2228736 | tf_op jit(solution)/shard_map/dot_general | solution.py:117
  72.8 3.9 %fusion.78 = (bf16[128,2304]{1,0:T(8,128)(2,1)S(1)}, f32[128,2304]{1,0:T(8,128)}) fusion(bf16[768,2304]{1,0:T(8,128)(2,1)} %all-gather.7.cloned.1.call-done, f32[128,768]{1,0:T(8,128)S(1)} %get-tuple-element.14, f32[128]{0:T(128)S(1)} %add_rsqrt_fusion, f32[128]{0:T(128)S(1)} %broadcast_multiply_fusion), kind=kOutput, calls=%fused_computation.120 | convolution fusion | flops 453574656 | bytes 5702656 | tf_op jit(solution)/shard_map/dot_general | solution.py:120
  76.7 16.6 %all_gather.21 = bf16[512,768]{1,0:T(8,128)(2,1)S(1)} all-gather(bf16[128,768]{1,0:T(8,128)(2,1)S(1)} %get-tuple-element.9), channel_id=1, replica_groups=mesh['groups'=2,'seq'=4,'mp'=2,'section'=2] {'seq'}, dimensions={0}, use_global_device_ids=true | all-gather | bytes 983040 | tf_op jit(solution)/shard_map/all_gather | solution.py:132
  93.5 1.0 fusion.52
  94.7 17.0 %all_gather.22 = bf16[512,768]{1,0:T(8,128)(2,1)S(1)} all-gather(bf16[128,768]{1,0:T(8,128)(2,1)S(1)} %get-tuple-element.10), channel_id=1, replica_groups=mesh['groups'=2,'seq'=4,'mp'=2,'section'=2] {'seq'}, dimensions={0}, use_global_device_ids=true | all-gather | bytes 983040 | tf_op jit(solution)/shard_map/all_gather | solution.py:133
  112.0 1.6 %fusion.3 = (f32[128,12]{0,1:T(8,128)S(1)}, f32[12,512,128]{2,1,0:T(8,128)S(1)}) fusion(pred[128,512]{0,1:T(8,128)(4,1)} %fusion.55, bf16[512,12,64]{0,2,1:T(8,128)(2,1)S(1)} %bitcast.113, bf16[128,12,64]{0,2,1:T(8,128)(2,1)S(1)} %bitcast.119), kind=kOutput, calls=%fused_computation.10 | convolution fusion | flops 102234624 | bytes 4200448 | tf_op jit(solution)/shard_map/qhd,khd->qhk/dot_general | solution.py:56
  113.6 0.7 fusion.11
  114.3 1.0 fusion.43
  115.3 2.3 %fusion.36 = bf16[1,128,768]{2,1,0:T(8,128)(2,1)} fusion(f32[128,768]{1,0:T(8,128)S(1)} %get-tuple-element.14, bf16[128,768]{0,1:T(8,128)(2,1)S(1)} %bitcast.121, bf16[768,768]{1,0:T(8,128)(2,1)} %all-gather.9.cloned.1.call-done), kind=kOutput, calls=%fused_computation.40 | convolution fusion | flops 151191552 | bytes 1966080 | tf_op jit(solution)/shard_map/dot_general | solution.py:137
  (65 shorter events, 5.8 us)
Async XLA Ops:
  7.4 40.7 %copy-start = (bf16[3,3,128,256]{3,2,1,0:T(8,128)(2,1)S(1)}, bf16[3,3,128,256]{3,2,1,0:T(8,128)(2,1)}, u32[]{:S(2)}) copy-start(bf16[3,3,128,256]{3,2,1,0:T(8,128)(2,1)} %param.10) | copy-start | bytes 1769476
  7.4 10.8 %copy-start.1 = (s32[1,512]{1,0:T(1,128)S(1)}, s32[1,512]{1,0:T(1,128)}, u32[]{:S(2)}) copy-start(s32[1,512]{1,0:T(1,128)} %param.14) | copy-start | bytes 6148
  7.4 15.2 %copy-start.2 = (bf16[1,64,8,1024]{3,2,1,0:T(8,128)(2,1)S(1)}, bf16[1,64,8,1024]{3,2,1,0:T(8,128)(2,1)}, u32[]{:S(2)}) copy-start(bf16[1,64,8,1024]{3,2,1,0:T(8,128)(2,1)} %param.8) | copy-start | bytes 3145732
  7.4 10.9 %top_k.24.cloned.1.call-start = ((), (), s32[]{:S(2)}) async-start(), calls=%async_computation.4 | async-start | bytes 12320 | tf_op jit(solution)/shard_map/top_k | solution.py:107
  9.4 61.3 %all-gather.5.cloned.1.call-start = ((), (), s32[]{:S(2)}) async-start(), calls=%async_computation.1 | async-start | bytes 1966080 | tf_op jit(solution)/shard_map/all_gather | solution.py:90
  10.0 62.8 %all-gather.7.cloned.1.call-start = ((), (), s32[]{:S(2)}) async-start(), calls=%async_computation.2 | async-start | bytes 4423680 | tf_op jit(solution)/shard_map/all_gather | solution.py:91
  10.6 104.8 %all-gather.9.cloned.1.call-start = ((), (), s32[]{:S(2)}) async-start(), calls=%async_computation.3 | async-start | bytes 1474560 | tf_op jit(solution)/shard_map/all_gather | solution.py:92
  12.1 10.5 %collective-permute-start = (bf16[64,1,1024]{2,1,0:T(2,128)(2,1)S(1)}, bf16[64,1,1024]{2,1,0:T(2,128)(2,1)S(1)}, u32[]{:S(2)}, u32[]{:S(2)}) collective-permute-start(bf16[64,1,1024]{2,1,0:T(2,128)(2,1)S(1)} %slice.34), channel_id=1, source_target_pairs={{0,4},{4,8},{8,12},{1,5},{5,9},{9,13},{2,6},{6,10},{10,14},{3,7},{... | collective-permute-start | bytes 393224 | tf_op jit(solution)/shard_map/ppermute | solution.py:16
  29.7 6.0 %copy-start.4 = (bf16[3,3,64,128]{3,2,1,0:T(8,128)(2,1)S(1)}, bf16[3,3,64,128]{3,2,1,0:T(8,128)(2,1)}, u32[]{:S(2)}) copy-start(bf16[3,3,64,128]{3,2,1,0:T(8,128)(2,1)} %param.9) | copy-start | bytes 442372
  29.7 6.1 %copy-start.6 = (pred[8,65]{0,1:T(8,128)(4,1)S(1)}, pred[8,65]{0,1:T(8,128)(4,1)}, u32[]{:S(2)}) copy-start(pred[8,65]{0,1:T(8,128)(4,1)} %constant.110) | copy-start | bytes 1564
  38.0 9.0 %collective-permute-start.1 = (bf16[128,1,512]{0,1,2:T(2,128)(2,1)S(1)}, bf16[128,1,512]{0,1,2:T(2,128)(2,1)S(1)}, u32[]{:S(2)}, u32[]{:S(2)}) collective-permute-start(bf16[128,1,512]{0,1,2:T(2,128)(2,1)S(1)} %slice.37), channel_id=1, source_target_pairs={{0,4},{4,8},{8,12},{1,5},{5,9},{9,13},{2,6},{6,10},{10,14},{3,7},{... | collective-permute-start | bytes 393224 | tf_op jit(solution)/shard_map/ppermute | solution.py:16
  47.6 0.7 copy-start.7
  49.5 7.9 %copy-start.5 = (s32[1,128]{1,0:T(1,128)S(1)}, s32[1,128]{1,0:T(1,128)}, u32[]{:S(2)}) copy-start(s32[1,128]{1,0:T(1,128)} %param.15) | copy-start | bytes 1540
  51.7 18.1 %all-to-all-start = ((bf16[4,32,1024]{2,1,0:T(8,128)(2,1)}), bf16[4,32,1024]{2,1,0:T(8,128)(2,1)S(1)}, u32[]{:S(2)}, u32[]{:S(2)}) async-start(bf16[4,32,1024]{2,1,0:T(8,128)(2,1)} %bitcast.19), calls=%async_computation | async-start | bytes 524288 | tf_op jit(solution)/shard_map/all_to_all | solution.py:115
  112.0 1.6 %copy-start.3 = (pred[128,512]{0,1:T(8,128)(4,1)S(1)}, pred[128,512]{0,1:T(8,128)(4,1)}, u32[]{:S(2)}) copy-start(pred[128,512]{0,1:T(8,128)(4,1)} %fusion.55) | copy-start | bytes 196612
Sparse Core Ops, SparseCore 0:
  10.4 2.2 top_k.26.cloned.1.call-done
  (1 shorter events, 0.0 us)
Sparse Core Ops, SparseCore 1:
  11.5 22.2 all-gather.4
  35.2 30.6 all-gather.6
  67.4 17.3 all-gather.8
where the time goes:
time: 126 us; the launch traced here: 125 us
  blocking collectives  45.1 us (36%)
  local copies, waits for them, and re-layouts  20.1 us (16%)
  between operations  15.4 us (12%)
  starting transfers between devices  15.2 us (12%)
  matrix products  12.2 us (10%)
  other arithmetic  10.3 us (8%)
  waiting for transfers between devices  6.94 us (6%)
    all_gather x1, blocking collectives, body(): lax.all_gather(values_flat, 'seq', axis=0, tiled=True)  17 us
    all_gather x1, blocking collectives, body(): lax.all_gather(keys_flat, 'seq', axis=0, tiled=True)  16.6 us
    all_gather x1, blocking collectives, body(): lax.all_gather(flags, 'seq', axis=0, tiled=True)  11.5 us
    conv_general_dilated x8, local copies, waits for them, and re-layouts, strided_conv(): lax.conv_general_dilated(padded[None], kernel, (2, 2), 'VALID', dimension...  11.4 us
    ppermute x2, starting transfers between devices, shifted(): lax.ppermute(value, axis, [(source, source + steps) for source in range(f...  9.34 us
    ppermute x2, waiting for transfers between devices, shifted(): lax.ppermute(value, axis, [(source, source + steps) for source in range(f...  5.79 us
    all_to_all x1, starting transfers between devices, body(): lax.all_to_all(outgoing, 'seq', split_axis=0, concat_axis=0, tiled=True)  5.78 us
    dot_general x1, matrix products, body(): jnp.dot(normed, project_full, preferred_element_type=jnp.float32)  3.86 us
  transfers between devices with their start and end apart: 6, of which 2 were waited for; matrix products, arithmetic and copies ran while one was open for 30% of the time, Pallas kernels for 0%

commit v1 on v0

v1 whole, which is shorter than its diff:
```python
import functools

import jax
import jax.numpy as jnp
from jax import lax
from jax.experimental import pallas as pl
from jax.experimental.pallas import tpu as pltpu
from jax.sharding import PartitionSpec as P

HEADS = 12
epsilon = 1e-05
MESH = pl.DeviceIdType.MESH
F32 = jnp.float32
BF16 = jnp.bfloat16


def silu(v):
    return v / (1.0 + jnp.exp(-v))


def normalize(tokens):
    values = tokens.astype(F32)
    center = jnp.mean(values, axis=-1, keepdims=True)
    spread = jnp.mean(jnp.square(values - center), axis=-1, keepdims=True)
    return ((values - center) * lax.rsqrt(spread + epsilon)).astype(BF16)


def dot(a, b):
    return jnp.dot(a, b, preferred_element_type=F32)


def kernel(
    sizes,
    x_ref, k1_ref, k2_ref, order_ref, active_ref, embed_ref, project_ref, output_ref,
    out_ref,
    we_ref, wp_ref, wo_ref, hx_ref, h1_ref, s1_ref, p0_ref, p1_ref, p2_ref, f_ref, g_ref,
    tok_ref, kv_ref, flag_ref,
    local_sem, mate_send, mate_recv, x_send, x_recv, y_send, y_recv,
    fwd_send, fwd_recv, halo_send, halo_recv, tok_send, tok_recv, flag_send, flag_recv,
):
    n, n_mp = sizes
    g, s = lax.axis_index("groups"), lax.axis_index("seq")
    m, c = lax.axis_index("mp"), lax.axis_index("section")
    mate = {"section": 1 - c}
    across = {"groups": 1 - g}

    def mp_peer(d):
        return {"mp": lax.rem(m + d, n_mp)}

    def seq_peer(d):
        return {"seq": lax.rem(s + d, n)}

    def remote(src, dst, send, recv, where):
        return pltpu.make_async_remote_copy(
            src_ref=src, dst_ref=dst, send_sem=send, recv_sem=recv, device_id=where, device_id_type=MESH
        )

    barrier = pltpu.get_barrier_semaphore()
    peers = [mate, across] + [mp_peer(d) for d in range(1, n_mp)] + [seq_peer(d) for d in range(1, n)]
    for where in peers:
        pl.semaphore_signal(barrier, inc=1, device_id=where, device_id_type=MESH)
    pl.semaphore_wait(barrier, len(peers))

    shards = (embed_ref, project_ref, output_ref)
    full = (we_ref, wp_ref, wo_ref)

    def half(ref, w, which):
        if w == 0:
            return ref.at[pl.ds(2 * which, 2)]
        cols = ref.shape[-1] // 2
        return ref.at[:, pl.ds(pl.multiple_of(which * cols, 128), cols)]

    def copy_local(w):
        return pltpu.make_async_copy(shards[w], full[w].at[m, c], local_sem.at[w])

    def copy_mate(w):
        return remote(shards[w], full[w].at[m, c], mate_send.at[w], mate_recv.at[w], mate)

    def copy_x(w, d):
        return remote(
            half(shards[w], w, g), half(full[w].at[m, c], w, g), x_send.at[w, d - 1], x_recv.at[w, d - 1], mp_peer(d)
        )

    def piece(w, d, which):
        return half(full[w].at[lax.rem(m + n_mp - d, n_mp), c], w, which)

    def copy_y(w, d):
        ref = piece(w, d, g)
        return remote(ref, ref, y_send.at[w, d - 1], y_recv.at[w, d - 1], across)

    def copy_fwd(w, d, k):
        ref = piece(w, d, g if k == 0 else 1 - g)
        return remote(ref, ref, fwd_send.at[w, d - 1, k], fwd_recv.at[w, d - 1, k], mate)

    steps = range(1, n_mp)

    def send_weight(w):
        for d in steps:
            copy_x(w, d).start()
        copy_mate(w).start()
        copy_local(w).start()

    def pass_x(w):
        for d in steps:
            copy_x(w, d).wait_recv()
            copy_y(w, d).start()
            copy_fwd(w, d, 0).start()

    def pass_y(w):
        for d in steps:
            copy_y(w, d).wait_recv()
            copy_fwd(w, d, 1).start()

    def finish_weight(w):
        copy_local(w).wait()
        copy_mate(w).wait_recv()
        for d in steps:
            copy_fwd(w, d, 0).wait_recv()
            copy_fwd(w, d, 1).wait_recv()

    def copy_halo(k):
        src, dst = ((x_ref.at[x_ref.shape[0] - 1], hx_ref), (s1_ref, h1_ref))[k]
        return remote(src, dst, halo_send.at[k], halo_recv.at[k], seq_peer(1))

    def start_halo(k):
        @pl.when(s < n - 1)
        def _():
            copy_halo(k).start()

    def await_halo(k, ref):
        @pl.when(s > 0)
        def _():
            copy_halo(k).wait_recv()

        @pl.when(s == 0)
        def _():
            ref[...] = jnp.zeros_like(ref)

    def copy_flag(d):
        ref = flag_ref.at[s]
        return remote(ref, ref, flag_send.at[d - 1], flag_recv.at[d - 1], seq_peer(d))

    def copy_tok(d):
        ref = tok_ref.at[s]
        return remote(ref, ref, tok_send.at[d - 1], tok_recv.at[d - 1], seq_peer(d))

    start_halo(0)
    send_weight(0)
    flag_ref[s] = jnp.broadcast_to(active_ref[...].astype(F32), flag_ref.shape[1:]).astype(BF16)
    for d in range(1, n):
        copy_flag(d).start()

    ticks = x_ref.shape[2]
    half_ticks, quarter = ticks // 2, ticks // 4
    for ref in (p0_ref, p1_ref, p2_ref):
        ref[0:8, :] = jnp.zeros((8, ref.shape[1]), F32)
    rows1 = x_ref.shape[0] // 2
    for w in range(rows1 + 1):
        f_ref[w, 0:8, :] = jnp.zeros((8, f_ref.shape[2]), F32)
    c_in, c_mid = k1_ref.shape[2], k1_ref.shape[3]
    k1 = jnp.concatenate([k1_ref[:, kw].reshape(3 * c_in, c_mid) for kw in range(3)], axis=1)

    def conv_one(w):
        low = hx_ref[...] if w == 0 else x_ref[2 * w - 1]
        rows = jnp.concatenate([low, x_ref[2 * w], x_ref[2 * w + 1]], axis=0)
        made = lax.dot_general(rows, k1, (((0,), (0,)), ((), ())), preferred_element_type=F32)
        for kw, ref in enumerate((p0_ref, p1_ref, p2_ref)):
            ref[8 : 8 + ticks, :] = made[:, kw * c_mid : (kw + 1) * c_mid]
        total = (
            p0_ref[pl.ds(7, half_ticks, stride=2), :]
            + p1_ref[pl.ds(8, half_ticks, stride=2), :]
            + p2_ref[pl.ds(9, half_ticks, stride=2), :]
        )
        result = silu(total).astype(BF16)
        f_ref[w + 1, 8 : 8 + half_ticks, :] = result.astype(F32)
        return result

    s1_ref[...] = conv_one(rows1 - 1)
    start_halo(1)
    send_weight(1)
    for w in range(1, rows1 - 1):
        conv_one(w)
    pass_x(0)
    await_halo(0, hx_ref)
    conv_one(0)
    send_weight(2)
    await_halo(1, h1_ref)
    f_ref[0, 8 : 8 + half_ticks, :] = h1_ref[...].astype(F32)
    pass_y(0)

    for w in range(rows1 // 2):
        parts = [
            f_ref[2 * w + kh, pl.ds(7 + kw, quarter, stride=2), :].astype(BF16) for kh in range(3) for kw in range(3)
        ]
        result = silu(dot(jnp.concatenate(parts, axis=1), k2_ref[...])).astype(BF16).astype(F32)
        g_ref[w, 0] = result[:, :128]
        g_ref[w, 1] = result[:, 128:]
    count = quarter // 2
    finish_weight(0)
    tokens = None
    for w in range(2):
        for t in range(2):
            rows = jnp.concatenate([g_ref[w, k, pl.ds(t, count, stride=2), :] for k in range(2)], axis=1)
            part = we_ref[:, :, 2 * w + t].reshape(rows.shape[1], we_ref.shape[4])
            term = dot(rows.astype(BF16), part)
            tokens = term if tokens is None else tokens + term
    tok_ref[s] = tokens.astype(BF16)
    for d in range(1, n):
        copy_tok(d).start()
    pass_x(1)

    total_len = n * count
    lanes = lax.broadcasted_iota(jnp.int32, (count, total_len), 1)
    for d in range(1, n):
        copy_flag(d).wait_recv()

    def activity(k, row):
        block = order_ref[pl.ds(pl.multiple_of(k * count, count), count), :]
        return row + dot(flag_ref[k], jnp.where(lanes == block, 1.0, 0.0).astype(BF16))

    row = lax.fori_loop(0, n, activity, jnp.zeros((flag_ref.shape[1], total_len), F32))
    own = lanes == order_ref[pl.ds(pl.multiple_of(s * count, count), count), :]
    onehot = jnp.where(own, 1.0, 0.0).astype(BF16)
    bias = jnp.where((row[0:1, :] > 0.5) | own, 0.0, -jnp.inf)

    pass_x(2)
    pass_y(1)
    finish_weight(1)
    width = wo_ref.shape[3]

    def place(k):
        normed = normalize(tok_ref[k])
        made = dot(normed, wp_ref[:, :, :, width:].reshape(width, 2 * width))
        kv_ref[pl.ds(pl.multiple_of(k * count, count), count), :] = made.astype(BF16)

    place(s)
    pass_y(2)

    def arrive(d, carry):
        copy_tok(d).wait_recv()
        place(lax.rem(s + n - d, n))
        return carry

    lax.fori_loop(1, n, arrive, 0)
    mine = dot(onehot, tok_ref[...].reshape(total_len, width)).astype(BF16)
    head = width // HEADS
    query = dot(normalize(mine), wp_ref[:, :, :, :width].reshape(width, width))
    query = (query * head ** (-0.5)).astype(BF16)
    low_half = lax.broadcasted_iota(jnp.int32, (count, 2 * head), 1) < head
    bias = jnp.concatenate([bias, bias], axis=0)
    mixed = []
    for h in range(HEADS // 2):
        cols = slice(h * 2 * head, (h + 1) * 2 * head)
        pair = query[:, cols]
        zero = jnp.zeros_like(pair)
        both = jnp.concatenate([jnp.where(low_half, pair, zero), jnp.where(low_half, zero, pair)], axis=0)
        keys = kv_ref[:, cols]
        values = kv_ref[:, slice(width + h * 2 * head, width + (h + 1) * 2 * head)]
        scores = lax.dot_general(both, keys, (((1,), (1,)), ((), ())), preferred_element_type=F32) + bias
        weights = jnp.exp(scores - jnp.max(scores, axis=-1, keepdims=True))
        total = jnp.sum(weights, axis=-1, keepdims=True)
        result = dot(weights.astype(BF16), values) / total
        mixed.append(jnp.where(low_half, result[:count], result[count:]).astype(BF16))
    finish_weight(2)
    final = mine.astype(F32) + dot(jnp.concatenate(mixed, axis=1), wo_ref[...].reshape(width, width))
    out_ref[...] = final.astype(BF16)

    for w in range(3):
        copy_mate(w).wait_send()
        for d in steps:
            copy_x(w, d).wait_send()
            copy_y(w, d).wait_send()
            copy_fwd(w, d, 0).wait_send()
            copy_fwd(w, d, 1).wait_send()
    for d in range(1, n):
        copy_flag(d).wait_send()
        copy_tok(d).wait_send()

    @pl.when(s < n - 1)
    def _():
        copy_halo(0).wait_send()
        copy_halo(1).wait_send()


def body(
    readout, first_kernel, second_kernel, embed_weight, project_weight, output_weight, order, active
):
    n, n_mp, n_sec = lax.axis_size("seq"), lax.axis_size("mp"), lax.axis_size("section")
    x = readout[0].transpose(1, 0, 2)
    wires, c_in, ticks = x.shape
    c_mid, c_out = second_kernel.shape[2:]
    width = embed_weight.shape[1]
    rows_e = embed_weight.shape[0] // 4
    embed = embed_weight.reshape(rows_e, 4, width).transpose(1, 0, 2)
    rows_p = project_weight.shape[0]
    count = active.shape[1]
    k2 = second_kernel.reshape(9 * c_mid, c_out)
    vmem = pl.BlockSpec(memory_space=pltpu.VMEM)
    hbm = pl.BlockSpec(memory_space=pl.ANY)
    dma = pltpu.SemaphoreType.DMA
    links = (3, n_mp - 1)
    result = pl.pallas_call(
        functools.partial(kernel, (n, n_mp)),
        out_shape=jax.ShapeDtypeStruct((count, width), BF16),
        in_specs=[vmem] * 5 + [hbm] * 3,
        out_specs=vmem,
        scratch_shapes=[
            pltpu.VMEM((n_mp, n_sec, 4, rows_e, width), BF16),
            pltpu.VMEM((n_mp, n_sec, rows_p, 3 * width), BF16),
            pltpu.VMEM((n_mp, n_sec, rows_p, width), BF16),
            pltpu.VMEM((c_in, ticks), BF16),
            pltpu.VMEM((ticks // 2, c_mid), BF16),
            pltpu.VMEM((ticks // 2, c_mid), BF16),
            pltpu.VMEM((ticks + 16, c_mid), F32),
            pltpu.VMEM((ticks + 16, c_mid), F32),
            pltpu.VMEM((ticks + 16, c_mid), F32),
            pltpu.VMEM((wires // 2 + 1, ticks // 2 + 16, c_mid), F32),
            pltpu.VMEM((wires // 4, 2, ticks // 4, c_out // 2), F32),
            pltpu.VMEM((n, count, width), BF16),
            pltpu.VMEM((n * count, 2 * width), BF16),
            pltpu.VMEM((n, 16, count), BF16),
            dma((3,)), dma((3,)), dma((3,)), dma(links), dma(links), dma(links), dma(links),
            dma(links + (2,)), dma(links + (2,)), dma((2,)), dma((2,)),
            dma((n - 1,)), dma((n - 1,)), dma((n - 1,)), dma((n - 1,)),
        ],
        compiler_params=pltpu.CompilerParams(
            collective_id=0, has_side_effects=True, vmem_limit_bytes=52 * 2**20
        ),
    )(x, first_kernel, k2, order[0][:, None], active, embed, project_weight, output_weight)
    return result[None]


def solution(mesh):
    in_specs = (
        P(("groups", "mp", "section"), None, "seq", None),
        P(),
        P(),
        P(("mp", "section"), None),
        P(("mp", "section"), None),
        P(("mp", "section"), None),
        P(("groups", "mp", "section"), None),
        P(("groups", "mp", "section"), "seq"),
    )
    out_specs = P(("groups", "mp", "section"), "seq", None)
    return jax.shard_map(body, mesh=mesh, in_specs=in_specs, out_specs=out_specs, check_vma=False)
```

time: 126 us -> 46.8 us (0.37)
  blocking collectives: 45.1 us -> 0 us
  Pallas kernels: 0 us -> 41.3 us
  between operations: 15.4 us -> 0.07 us
  local copies, waits for them, and re-layouts: 20.1 us -> 4.86 us
  starting transfers between devices: 15.2 us -> 0 us
  matrix products: 12.2 us -> 0 us
  other arithmetic: 10.3 us -> 0 us
  waiting for transfers between devices: 6.94 us -> 0 us
    all_gather x3 -> x0, blocking collectives: 45.1 us -> none  [the longest x1 17 us: body(): lax.all_gather(values_flat, 'seq', axis=0, tiled=True)]
    pallas_call x0 -> x1, Pallas kernels: none -> 41.3 us  [body(): pl.pallas_call(functools.partial(kernel, (n, n_mp)), out_shape=jax.ShapeD...]
    conv_general_dilated x8 -> x0, local copies, waits for them, and re-layouts: 11.4 us -> none  [strided_conv(): lax.conv_general_dilated(padded[None], kernel, (2, 2), 'VALID', dimension...]
    dot_general x5 -> x0, matrix products: 10.6 us -> none  [the longest x1 3.86 us: body(): jnp.dot(normed, project_full, preferred_element_type=jnp.float32)]
    ppermute x2 -> x0, starting transfers between devices: 9.34 us -> none  [shifted(): lax.ppermute(value, axis, [(source, source + steps) for source in range(f...]
    ppermute x2 -> x0, waiting for transfers between devices: 5.79 us -> none  [shifted(): lax.ppermute(value, axis, [(source, source + steps) for source in range(f...]
    all_to_all x1 -> x0, starting transfers between devices: 5.78 us -> none  [body(): lax.all_to_all(outgoing, 'seq', split_axis=0, concat_axis=0, tiled=True)]
    gather x5 -> x0, local copies, waits for them, and re-layouts: 4.09 us -> none  [the longest x3 1.67 us: body(): jnp.take_along_axis(blocks, picked, axis=1) % count]
  transfers between devices with their start and end apart: 6 -> 0, of which waited for: 2 -> 0; matrix products, arithmetic and copies ran while one was open for 30% -> 0% of each run, Pallas kernels for 0% -> 0%
where the time goes in v1:
time: 46.8 us; the launch traced here: 46.2 us
  Pallas kernels  41.3 us (88%)
  local copies, waits for them, and re-layouts  4.86 us (10%)
    pallas_call x1, Pallas kernels, body(): pl.pallas_call(functools.partial(kernel, (n, n_mp)), out_shape=jax.ShapeD...  41.3 us
    unnamed x14, local copies, waits for them, and re-layouts  3.58 us
    reshape x2, local copies, waits for them, and re-layouts, body(): embed = embed_weight.reshape(rows_e, 4, width).transpose(1, 0, 2)  1.14 us

profile of v1, /device:TPU:0, one launch (start us, length us, event | category | flops | bytes accessed | tf_op | source)
XLA Modules:
  0.0 46.2 jit_solution(15508947281309999742)
XLA Ops:
  0.0 0.0 copy-start.5
  0.0 0.0 copy-start.4
  0.0 0.7 %copy-done.5 = s32[1,512]{1,0:T(1,128)S(1)} copy-done((s32[1,512]{1,0:T(1,128)S(1)}, s32[1,512]{1,0:T(1,128)}, u32[]{:S(2)}) %copy-start.5) | copy-done | bytes 2072
  0.7 0.1 copy.12.order_ref
  0.8 1.1 %reshape.7 = bf16[64,4,768]{2,1,0:T(4,128)(2,1)S(1)} reshape(bf16[256,768]{1,0:T(8,128)(2,1)} %param.11) | data formatting | bytes 786432 | tf_op jit(solution)/shard_map/reshape | solution.py:294
  2.0 0.0 copy-done.4
  2.0 0.0 copy-start
  2.0 0.0 copy-start.1
  2.0 0.0 copy-start.2
  2.0 1.6 %copy.15 = bf16[1,64,8,1024]{3,1,2,0:T(8,128)(2,1)} copy(bf16[1,64,8,1024]{3,2,1,0:T(8,128)(2,1)S(1)} %copy-done.4) | data formatting | bytes 2097152 | tf_op args[0]
  3.6 0.0 copy-start.3
  3.6 0.0 copy-done
  3.6 0.0 copy-done.1
  3.6 0.0 copy-done.2
  3.6 0.6 %copy-done.3 = s32[1,128]{1,0:T(1,128)S(1)} copy-done((s32[1,128]{1,0:T(1,128)S(1)}, s32[1,128]{1,0:T(1,128)}, u32[]{:S(2)}) %copy-start.3) | copy-done | bytes 536
  4.2 41.3 %shard_map.82 = bf16[128,768]{1,0:T(8,128)(2,1)S(1)} custom-call(bf16[8,64,1024]{2,1,0:T(8,128)(2,1)} %bitcast.14, bf16[3,3,64,128]{3,2,1,0:T(8,128)(2,1)S(1)} %copy-done.2, bf16[1152,256]{1,0:T(8,128)(2,1)S(1)} %bitcast.13, s32[512,1]{1,0:T(8,128)S(1)} %copy.12.order_ref, s32[1,128]{1,0:T(1,128)S(1)} %copy-done.3, bf16[4,64,768]{2,1,0:T(8,128)(2,1)S(1)} %bitcast.11, ...), custom_call_target="tpu_custom_call" | custom-call | tf_op jit(solution)/shard_map/pallas_call | solution.py:302
  45.5 0.7 %copy.18 = bf16[1,128,768]{2,1,0:T(8,128)(2,1)} copy(bf16[1,128,768]{2,1,0:T(8,128)(2,1)S(1)} %bitcast.12) | data formatting | bytes 393216
  (1 shorter events, 0.0 us)
Async XLA Ops:
  0.0 0.7 %copy-start.5 = (s32[1,512]{1,0:T(1,128)S(1)}, s32[1,512]{1,0:T(1,128)}, u32[]{:S(2)}) copy-start(s32[1,512]{1,0:T(1,128)} %param.14) | copy-start | bytes 6148
  0.0 2.0 %copy-start.4 = (bf16[1,64,8,1024]{3,2,1,0:T(8,128)(2,1)S(1)}, bf16[1,64,8,1024]{3,2,1,0:T(8,128)(2,1)}, u32[]{:S(2)}) copy-start(bf16[1,64,8,1024]{3,2,1,0:T(8,128)(2,1)} %param.8) | copy-start | bytes 3145732
  2.0 1.6 %copy-start = (bf16[3,3,128,256]{3,2,1,0:T(8,128)(2,1)S(1)}, bf16[3,3,128,256]{3,2,1,0:T(8,128)(2,1)}, u32[]{:S(2)}) copy-start(bf16[3,3,128,256]{3,2,1,0:T(8,128)(2,1)} %param.10) | copy-start | bytes 1769476
  2.0 1.6 %copy-start.1 = (bf16[192,768]{1,0:T(8,128)(2,1)S(1)}, bf16[192,768]{1,0:T(8,128)(2,1)}, u32[]{:S(2)}) copy-start(bf16[192,768]{1,0:T(8,128)(2,1)} %output_ref.1) | copy-start | bytes 884740
  2.0 1.6 %copy-start.2 = (bf16[3,3,64,128]{3,2,1,0:T(8,128)(2,1)S(1)}, bf16[3,3,64,128]{3,2,1,0:T(8,128)(2,1)}, u32[]{:S(2)}) copy-start(bf16[3,3,64,128]{3,2,1,0:T(8,128)(2,1)} %k1_ref.1) | copy-start | bytes 442372
  3.6 0.7 %copy-start.3 = (s32[1,128]{1,0:T(1,128)S(1)}, s32[1,128]{1,0:T(1,128)}, u32[]{:S(2)}) copy-start(s32[1,128]{1,0:T(1,128)} %active_ref.1) | copy-start | bytes 1540

commit v2 on v1

--- a/solution.py
+++ b/solution.py
@@ -61,20 +61,25 @@
         pl.semaphore_signal(barrier, inc=1, device_id=where, device_id_type=MESH)
     pl.semaphore_wait(barrier, len(peers))
 
-    shards = (embed_ref, project_ref, output_ref)
-    full = (we_ref, wp_ref, wo_ref)
+    width = wo_ref.shape[3]
+    shards = (embed_ref, project_ref, project_ref, output_ref)
+    full = (we_ref, wp_ref, wp_ref, wo_ref)
+    spans = (None, (width, 2 * width), (0, width), (0, width))
 
     def half(ref, w, which):
         if w == 0:
             return ref.at[pl.ds(2 * which, 2)]
-        cols = ref.shape[-1] // 2
-        return ref.at[:, pl.ds(pl.multiple_of(which * cols, 128), cols)]
+        base, cols = spans[w][0], spans[w][1] // 2
+        return ref.at[:, pl.ds(pl.multiple_of(base + which * cols, 128), cols)]
+
+    def span(ref, w):
+        return ref if w == 0 else ref.at[:, pl.ds(*spans[w])]
 
     def copy_local(w):
-        return pltpu.make_async_copy(shards[w], full[w].at[m, c], local_sem.at[w])
+        return pltpu.make_async_copy(span(shards[w], w), span(full[w].at[m, c], w), local_sem.at[w])
 
     def copy_mate(w):
-        return remote(shards[w], full[w].at[m, c], mate_send.at[w], mate_recv.at[w], mate)
+        return remote(span(shards[w], w), span(full[w].at[m, c], w), mate_send.at[w], mate_recv.at[w], mate)
 
     def copy_x(w, d):
         return remote(
@@ -140,9 +145,24 @@
         ref = flag_ref.at[s]
         return remote(ref, ref, flag_send.at[d - 1], flag_recv.at[d - 1], seq_peer(d))
 
-    def copy_tok(d):
-        ref = tok_ref.at[s]
-        return remote(ref, ref, tok_send.at[d - 1], tok_recv.at[d - 1], seq_peer(d))
+    def copy_tok(way, k):
+        ref = tok_ref.at[lax.rem(s + n - k if way == 0 else s + k, n)]
+        where = seq_peer(1 if way == 0 else n - 1)
+        return remote(ref, ref, tok_send.at[way, k], tok_recv.at[way, k], where)
+
+    def has(way, k):
+        return s >= k if way == 0 else s + k < n
+
+    def relay(k):
+        for way in range(2):
+
+            @pl.when(has(way, k))
+            def _(way=way):
+                copy_tok(way, k - 1).wait_recv()
+
+            @pl.when(has(way, k) & has(1 - way, 1))
+            def _(way=way):
+                copy_tok(way, k).start()
 
     start_halo(0)
     send_weight(0)
@@ -178,12 +198,13 @@
     s1_ref[...] = conv_one(rows1 - 1)
     start_halo(1)
     send_weight(1)
+    send_weight(2)
     for w in range(1, rows1 - 1):
         conv_one(w)
     pass_x(0)
     await_halo(0, hx_ref)
     conv_one(0)
-    send_weight(2)
+    send_weight(3)
     await_halo(1, h1_ref)
     f_ref[0, 8 : 8 + half_ticks, :] = h1_ref[...].astype(F32)
     pass_y(0)
@@ -205,8 +226,12 @@
             term = dot(rows.astype(BF16), part)
             tokens = term if tokens is None else tokens + term
     tok_ref[s] = tokens.astype(BF16)
-    for d in range(1, n):
-        copy_tok(d).start()
+    for way in range(2):
+
+        @pl.when(has(1 - way, 1))
+        def _(way=way):
+            copy_tok(way, 0).start()
+
     pass_x(1)
 
     total_len = n * count
@@ -223,10 +248,11 @@
     onehot = jnp.where(own, 1.0, 0.0).astype(BF16)
     bias = jnp.where((row[0:1, :] > 0.5) | own, 0.0, -jnp.inf)
 
+    pass_y(1)
+    relay(1)
     pass_x(2)
-    pass_y(1)
+    pass_x(3)
     finish_weight(1)
-    width = wo_ref.shape[3]
 
     def place(k):
         normed = normalize(tok_ref[k])
@@ -234,16 +260,27 @@
         kv_ref[pl.ds(pl.multiple_of(k * count, count), count), :] = made.astype(BF16)
 
     place(s)
+
+    def place_both(k):
+        for way in range(2):
+
+            @pl.when(has(way, k))
+            def _(way=way):
+                place(s - k if way == 0 else s + k)
+
+    def arrive(k, carry):
+        relay(k)
+        place_both(k)
+        return carry
+
+    if n > 1:
+        place_both(1)
     pass_y(2)
-
-    def arrive(d, carry):
-        copy_tok(d).wait_recv()
-        place(lax.rem(s + n - d, n))
-        return carry
-
-    lax.fori_loop(1, n, arrive, 0)
+    pass_y(3)
+    lax.fori_loop(2, n, arrive, 0)
     mine = dot(onehot, tok_ref[...].reshape(total_len, width)).astype(BF16)
     head = width // HEADS
+    finish_weight(2)
     query = dot(normalize(mine), wp_ref[:, :, :, :width].reshape(width, width))
     query = (query * head ** (-0.5)).astype(BF16)
     low_half = lax.broadcasted_iota(jnp.int32, (count, 2 * head), 1) < head
@@ -261,11 +298,11 @@
         total = jnp.sum(weights, axis=-1, keepdims=True)
         result = dot(weights.astype(BF16), values) / total
         mixed.append(jnp.where(low_half, result[:count], result[count:]).astype(BF16))
-    finish_weight(2)
+    finish_weight(3)
     final = mine.astype(F32) + dot(jnp.concatenate(mixed, axis=1), wo_ref[...].reshape(width, width))
     out_ref[...] = final.astype(BF16)
 
-    for w in range(3):
+    for w in range(4):
         copy_mate(w).wait_send()
         for d in steps:
             copy_x(w, d).wait_send()
@@ -274,7 +311,17 @@
             copy_fwd(w, d, 1).wait_send()
     for d in range(1, n):
         copy_flag(d).wait_send()
-        copy_tok(d).wait_send()
+
+    def drain(k, carry):
+        for way in range(2):
+
+            @pl.when(has(way, k) & has(1 - way, 1))
+            def _(way=way):
+                copy_tok(way, k).wait_send()
+
+        return carry
+
+    lax.fori_loop(0, n - 1, drain, 0)
 
     @pl.when(s < n - 1)
     def _():
@@ -298,7 +345,7 @@
     vmem = pl.BlockSpec(memory_space=pltpu.VMEM)
     hbm = pl.BlockSpec(memory_space=pl.ANY)
     dma = pltpu.SemaphoreType.DMA
-    links = (3, n_mp - 1)
+    links = (4, n_mp - 1)
     result = pl.pallas_call(
         functools.partial(kernel, (n, n_mp)),
         out_shape=jax.ShapeDtypeStruct((count, width), BF16),
@@ -319,9 +366,9 @@
             pltpu.VMEM((n, count, width), BF16),
             pltpu.VMEM((n * count, 2 * width), BF16),
             pltpu.VMEM((n, 16, count), BF16),
-            dma((3,)), dma((3,)), dma((3,)), dma(links), dma(links), dma(links), dma(links),
+            dma((4,)), dma((4,)), dma((4,)), dma(links), dma(links), dma(links), dma(links),
             dma(links + (2,)), dma(links + (2,)), dma((2,)), dma((2,)),
-            dma((n - 1,)), dma((n - 1,)), dma((n - 1,)), dma((n - 1,)),
+            dma((2, n)), dma((2, n)), dma((n - 1,)), dma((n - 1,)),
         ],
         compiler_params=pltpu.CompilerParams(
             collective_id=0, has_side_effects=True, vmem_limit_bytes=52 * 2**20

time: 46.8 us -> 51.7 us (1.10)
  Pallas kernels: 41.3 us -> 46.6 us
    pallas_call x1, Pallas kernels: 41.3 us -> 46.6 us  [body(): pl.pallas_call(functools.partial(kernel, (n, n_mp)), out_shape=jax.ShapeD...]
where the time goes in v2:
time: 51.7 us; the launch traced here: 51.5 us
  Pallas kernels  46.6 us (90%)
  local copies, waits for them, and re-layouts  4.86 us (9%)
    pallas_call x1, Pallas kernels, body(): pl.pallas_call(functools.partial(kernel, (n, n_mp)), out_shape=jax.ShapeD...  46.6 us
    unnamed x14, local copies, waits for them, and re-layouts  3.58 us
    reshape x2, local copies, waits for them, and re-layouts, body(): embed = embed_weight.reshape(rows_e, 4, width).transpose(1, 0, 2)  1.14 us

profile of v2, /device:TPU:0, one launch (start us, length us, event | category | flops | bytes accessed | tf_op | source)
XLA Modules:
  0.0 51.5 jit_solution(12825002375754659127)
XLA Ops:
  0.0 0.0 copy-start.5
  0.0 0.0 copy-start.4
  0.0 0.7 %copy-done.5 = s32[1,512]{1,0:T(1,128)S(1)} copy-done((s32[1,512]{1,0:T(1,128)S(1)}, s32[1,512]{1,0:T(1,128)}, u32[]{:S(2)}) %copy-start.5) | copy-done | bytes 2072
  0.7 0.1 copy.12.order_ref
  0.8 1.1 %reshape.7 = bf16[64,4,768]{2,1,0:T(4,128)(2,1)S(1)} reshape(bf16[256,768]{1,0:T(8,128)(2,1)} %param.11) | data formatting | bytes 786432 | tf_op jit(solution)/shard_map/reshape | solution.py:341
  2.0 0.0 copy-done.4
  2.0 0.0 copy-start
  2.0 0.0 copy-start.1
  2.0 0.0 copy-start.2
  2.0 1.6 %copy.15 = bf16[1,64,8,1024]{3,1,2,0:T(8,128)(2,1)} copy(bf16[1,64,8,1024]{3,2,1,0:T(8,128)(2,1)S(1)} %copy-done.4) | data formatting | bytes 2097152 | tf_op args[0]
  3.6 0.0 copy-start.3
  3.6 0.0 copy-done
  3.6 0.0 copy-done.1
  3.6 0.0 copy-done.2
  3.6 0.6 %copy-done.3 = s32[1,128]{1,0:T(1,128)S(1)} copy-done((s32[1,128]{1,0:T(1,128)S(1)}, s32[1,128]{1,0:T(1,128)}, u32[]{:S(2)}) %copy-start.3) | copy-done | bytes 536
  4.2 46.6 %shard_map.82 = bf16[128,768]{1,0:T(8,128)(2,1)S(1)} custom-call(bf16[8,64,1024]{2,1,0:T(8,128)(2,1)} %bitcast.14, bf16[3,3,64,128]{3,2,1,0:T(8,128)(2,1)S(1)} %copy-done.2, bf16[1152,256]{1,0:T(8,128)(2,1)S(1)} %bitcast.13, s32[512,1]{1,0:T(8,128)S(1)} %copy.12.order_ref, s32[1,128]{1,0:T(1,128)S(1)} %copy-done.3, bf16[4,64,768]{2,1,0:T(8,128)(2,1)S(1)} %bitcast.11, ...), custom_call_target="tpu_custom_call" | custom-call | tf_op jit(solution)/shard_map/pallas_call | solution.py:349
  50.8 0.7 %copy.18 = bf16[1,128,768]{2,1,0:T(8,128)(2,1)} copy(bf16[1,128,768]{2,1,0:T(8,128)(2,1)S(1)} %bitcast.12) | data formatting | bytes 393216
  (1 shorter events, 0.0 us)
Async XLA Ops:
  0.0 0.7 %copy-start.5 = (s32[1,512]{1,0:T(1,128)S(1)}, s32[1,512]{1,0:T(1,128)}, u32[]{:S(2)}) copy-start(s32[1,512]{1,0:T(1,128)} %param.14) | copy-start | bytes 6148
  0.0 2.0 %copy-start.4 = (bf16[1,64,8,1024]{3,2,1,0:T(8,128)(2,1)S(1)}, bf16[1,64,8,1024]{3,2,1,0:T(8,128)(2,1)}, u32[]{:S(2)}) copy-start(bf16[1,64,8,1024]{3,2,1,0:T(8,128)(2,1)} %param.8) | copy-start | bytes 3145732
  2.0 1.6 %copy-start = (bf16[3,3,128,256]{3,2,1,0:T(8,128)(2,1)S(1)}, bf16[3,3,128,256]{3,2,1,0:T(8,128)(2,1)}, u32[]{:S(2)}) copy-start(bf16[3,3,128,256]{3,2,1,0:T(8,128)(2,1)} %param.10) | copy-start | bytes 1769476
  2.0 1.6 %copy-start.1 = (bf16[192,768]{1,0:T(8,128)(2,1)S(1)}, bf16[192,768]{1,0:T(8,128)(2,1)}, u32[]{:S(2)}) copy-start(bf16[192,768]{1,0:T(8,128)(2,1)} %output_ref.1) | copy-start | bytes 884740
  2.0 1.6 %copy-start.2 = (bf16[3,3,64,128]{3,2,1,0:T(8,128)(2,1)S(1)}, bf16[3,3,64,128]{3,2,1,0:T(8,128)(2,1)}, u32[]{:S(2)}) copy-start(bf16[3,3,64,128]{3,2,1,0:T(8,128)(2,1)} %k1_ref.1) | copy-start | bytes 442372
  3.6 0.7 %copy-start.3 = (s32[1,128]{1,0:T(1,128)S(1)}, s32[1,128]{1,0:T(1,128)}, u32[]{:S(2)}) copy-start(s32[1,128]{1,0:T(1,128)} %active_ref.1) | copy-start | bytes 1540

commit v3 on v1

--- a/solution.py
+++ b/solution.py
@@ -61,20 +61,25 @@
         pl.semaphore_signal(barrier, inc=1, device_id=where, device_id_type=MESH)
     pl.semaphore_wait(barrier, len(peers))
 
-    shards = (embed_ref, project_ref, output_ref)
-    full = (we_ref, wp_ref, wo_ref)
+    width = wo_ref.shape[3]
+    shards = (embed_ref, project_ref, project_ref, output_ref)
+    full = (we_ref, wp_ref, wp_ref, wo_ref)
+    spans = (None, (width, 2 * width), (0, width), (0, width))
 
     def half(ref, w, which):
         if w == 0:
             return ref.at[pl.ds(2 * which, 2)]
-        cols = ref.shape[-1] // 2
-        return ref.at[:, pl.ds(pl.multiple_of(which * cols, 128), cols)]
+        base, cols = spans[w][0], spans[w][1] // 2
+        return ref.at[:, pl.ds(pl.multiple_of(base + which * cols, 128), cols)]
+
+    def span(ref, w):
+        return ref if w == 0 else ref.at[:, pl.ds(*spans[w])]
 
     def copy_local(w):
-        return pltpu.make_async_copy(shards[w], full[w].at[m, c], local_sem.at[w])
+        return pltpu.make_async_copy(span(shards[w], w), span(full[w].at[m, c], w), local_sem.at[w])
 
     def copy_mate(w):
-        return remote(shards[w], full[w].at[m, c], mate_send.at[w], mate_recv.at[w], mate)
+        return remote(span(shards[w], w), span(full[w].at[m, c], w), mate_send.at[w], mate_recv.at[w], mate)
 
     def copy_x(w, d):
         return remote(
@@ -178,12 +183,13 @@
     s1_ref[...] = conv_one(rows1 - 1)
     start_halo(1)
     send_weight(1)
+    send_weight(2)
     for w in range(1, rows1 - 1):
         conv_one(w)
     pass_x(0)
     await_halo(0, hx_ref)
     conv_one(0)
-    send_weight(2)
+    send_weight(3)
     await_halo(1, h1_ref)
     f_ref[0, 8 : 8 + half_ticks, :] = h1_ref[...].astype(F32)
     pass_y(0)
@@ -225,8 +231,8 @@
 
     pass_x(2)
     pass_y(1)
+    pass_x(3)
     finish_weight(1)
-    width = wo_ref.shape[3]
 
     def place(k):
         normed = normalize(tok_ref[k])
@@ -234,7 +240,9 @@
         kv_ref[pl.ds(pl.multiple_of(k * count, count), count), :] = made.astype(BF16)
 
     place(s)
+
     pass_y(2)
+    pass_y(3)
 
     def arrive(d, carry):
         copy_tok(d).wait_recv()
@@ -244,6 +252,7 @@
     lax.fori_loop(1, n, arrive, 0)
     mine = dot(onehot, tok_ref[...].reshape(total_len, width)).astype(BF16)
     head = width // HEADS
+    finish_weight(2)
     query = dot(normalize(mine), wp_ref[:, :, :, :width].reshape(width, width))
     query = (query * head ** (-0.5)).astype(BF16)
     low_half = lax.broadcasted_iota(jnp.int32, (count, 2 * head), 1) < head
@@ -261,11 +270,11 @@
         total = jnp.sum(weights, axis=-1, keepdims=True)
         result = dot(weights.astype(BF16), values) / total
         mixed.append(jnp.where(low_half, result[:count], result[count:]).astype(BF16))
-    finish_weight(2)
+    finish_weight(3)
     final = mine.astype(F32) + dot(jnp.concatenate(mixed, axis=1), wo_ref[...].reshape(width, width))
     out_ref[...] = final.astype(BF16)
 
-    for w in range(3):
+    for w in range(4):
         copy_mate(w).wait_send()
         for d in steps:
             copy_x(w, d).wait_send()
@@ -298,7 +307,7 @@
     vmem = pl.BlockSpec(memory_space=pltpu.VMEM)
     hbm = pl.BlockSpec(memory_space=pl.ANY)
     dma = pltpu.SemaphoreType.DMA
-    links = (3, n_mp - 1)
+    links = (4, n_mp - 1)
     result = pl.pallas_call(
         functools.partial(kernel, (n, n_mp)),
         out_shape=jax.ShapeDtypeStruct((count, width), BF16),
@@ -319,7 +328,7 @@
             pltpu.VMEM((n, count, width), BF16),
             pltpu.VMEM((n * count, 2 * width), BF16),
             pltpu.VMEM((n, 16, count), BF16),
-            dma((3,)), dma((3,)), dma((3,)), dma(links), dma(links), dma(links), dma(links),
+            dma((4,)), dma((4,)), dma((4,)), dma(links), dma(links), dma(links), dma(links),
             dma(links + (2,)), dma(links + (2,)), dma((2,)), dma((2,)),
             dma((n - 1,)), dma((n - 1,)), dma((n - 1,)), dma((n - 1,)),
         ],

time: 46.8 us -> 46.2 us (0.987)
  the two profiles are of different devices: /device:TPU:0 before, /device:TPU:25 now
where the time goes in v3:
time: 46.2 us; the launch traced here: 46 us
  Pallas kernels  41.1 us (89%)
  local copies, waits for them, and re-layouts  4.86 us (11%)
    pallas_call x1, Pallas kernels, body(): pl.pallas_call(functools.partial(kernel, (n, n_mp)), out_shape=jax.ShapeD...  41.1 us
    unnamed x14, local copies, waits for them, and re-layouts  3.58 us
    reshape x2, local copies, waits for them, and re-layouts, body(): embed = embed_weight.reshape(rows_e, 4, width).transpose(1, 0, 2)  1.14 us

profile of v3, /device:TPU:25, one launch (start us, length us, event | category | flops | bytes accessed | tf_op | source)
XLA Modules:
  0.0 46.0 jit_solution(5604518087842958774)
XLA Ops:
  0.0 0.0 copy-start.5
  0.0 0.0 copy-start.4
  0.0 0.7 %copy-done.5 = s32[1,512]{1,0:T(1,128)S(1)} copy-done((s32[1,512]{1,0:T(1,128)S(1)}, s32[1,512]{1,0:T(1,128)}, u32[]{:S(2)}) %copy-start.5) | copy-done | bytes 2072
  0.7 0.1 copy.12.order_ref
  0.8 1.1 %reshape.7 = bf16[64,4,768]{2,1,0:T(4,128)(2,1)S(1)} reshape(bf16[256,768]{1,0:T(8,128)(2,1)} %param.11) | data formatting | bytes 786432 | tf_op jit(solution)/shard_map/reshape | solution.py:303
  2.0 0.0 copy-done.4
  2.0 0.0 copy-start
  2.0 0.0 copy-start.1
  2.0 0.0 copy-start.2
  2.0 1.6 %copy.15 = bf16[1,64,8,1024]{3,1,2,0:T(8,128)(2,1)} copy(bf16[1,64,8,1024]{3,2,1,0:T(8,128)(2,1)S(1)} %copy-done.4) | data formatting | bytes 2097152 | tf_op args[0]
  3.6 0.0 copy-start.3
  3.6 0.0 copy-done
  3.6 0.0 copy-done.1
  3.6 0.0 copy-done.2
  3.6 0.6 %copy-done.3 = s32[1,128]{1,0:T(1,128)S(1)} copy-done((s32[1,128]{1,0:T(1,128)S(1)}, s32[1,128]{1,0:T(1,128)}, u32[]{:S(2)}) %copy-start.3) | copy-done | bytes 536
  4.2 41.1 %shard_map.82 = bf16[128,768]{1,0:T(8,128)(2,1)S(1)} custom-call(bf16[8,64,1024]{2,1,0:T(8,128)(2,1)} %bitcast.14, bf16[3,3,64,128]{3,2,1,0:T(8,128)(2,1)S(1)} %copy-done.2, bf16[1152,256]{1,0:T(8,128)(2,1)S(1)} %bitcast.13, s32[512,1]{1,0:T(8,128)S(1)} %copy.12.order_ref, s32[1,128]{1,0:T(1,128)S(1)} %copy-done.3, bf16[4,64,768]{2,1,0:T(8,128)(2,1)S(1)} %bitcast.11, ...), custom_call_target="tpu_custom_call" | custom-call | tf_op jit(solution)/shard_map/pallas_call | solution.py:311
  45.3 0.7 %copy.18 = bf16[1,128,768]{2,1,0:T(8,128)(2,1)} copy(bf16[1,128,768]{2,1,0:T(8,128)(2,1)S(1)} %bitcast.12) | data formatting | bytes 393216
  (1 shorter events, 0.0 us)
Async XLA Ops:
  0.0 0.7 %copy-start.5 = (s32[1,512]{1,0:T(1,128)S(1)}, s32[1,512]{1,0:T(1,128)}, u32[]{:S(2)}) copy-start(s32[1,512]{1,0:T(1,128)} %param.14) | copy-start | bytes 6148
  0.0 2.0 %copy-start.4 = (bf16[1,64,8,1024]{3,2,1,0:T(8,128)(2,1)S(1)}, bf16[1,64,8,1024]{3,2,1,0:T(8,128)(2,1)}, u32[]{:S(2)}) copy-start(bf16[1,64,8,1024]{3,2,1,0:T(8,128)(2,1)} %param.8) | copy-start | bytes 3145732
  2.0 1.6 %copy-start = (bf16[3,3,128,256]{3,2,1,0:T(8,128)(2,1)S(1)}, bf16[3,3,128,256]{3,2,1,0:T(8,128)(2,1)}, u32[]{:S(2)}) copy-start(bf16[3,3,128,256]{3,2,1,0:T(8,128)(2,1)} %param.10) | copy-start | bytes 1769476
  2.0 1.6 %copy-start.1 = (bf16[192,768]{1,0:T(8,128)(2,1)S(1)}, bf16[192,768]{1,0:T(8,128)(2,1)}, u32[]{:S(2)}) copy-start(bf16[192,768]{1,0:T(8,128)(2,1)} %output_ref.1) | copy-start | bytes 884740
  2.0 1.6 %copy-start.2 = (bf16[3,3,64,128]{3,2,1,0:T(8,128)(2,1)S(1)}, bf16[3,3,64,128]{3,2,1,0:T(8,128)(2,1)}, u32[]{:S(2)}) copy-start(bf16[3,3,64,128]{3,2,1,0:T(8,128)(2,1)} %k1_ref.1) | copy-start | bytes 442372
  3.6 0.7 %copy-start.3 = (s32[1,128]{1,0:T(1,128)S(1)}, s32[1,128]{1,0:T(1,128)}, u32[]{:S(2)}) copy-start(s32[1,128]{1,0:T(1,128)} %active_ref.1) | copy-start | bytes 1540

commit v4 on v3

--- a/solution.py
+++ b/solution.py
@@ -31,10 +31,10 @@
 
 def kernel(
     sizes,
-    x_ref, k1_ref, k2_ref, order_ref, active_ref, embed_ref, project_ref, output_ref,
+    raw_ref, k1_ref, k2_ref, order_ref, active_ref, embed_ref, project_ref, output_ref,
     out_ref,
     we_ref, wp_ref, wo_ref, hx_ref, h1_ref, s1_ref, p0_ref, p1_ref, p2_ref, f_ref, g_ref,
-    tok_ref, kv_ref, flag_ref,
+    tok_ref, kv_ref, flag_ref, x_ref, split_ref, act_ref, act_sem,
     local_sem, mate_send, mate_recv, x_send, x_recv, y_send, y_recv,
     fwd_send, fwd_recv, halo_send, halo_recv, tok_send, tok_recv, flag_send, flag_recv,
 ):
@@ -55,6 +55,8 @@
             src_ref=src, dst_ref=dst, send_sem=send, recv_sem=recv, device_id=where, device_id_type=MESH
         )
 
+    copy_act = pltpu.make_async_copy(active_ref, act_ref, act_sem)
+    copy_act.start()
     barrier = pltpu.get_barrier_semaphore()
     peers = [mate, across] + [mp_peer(d) for d in range(1, n_mp)] + [seq_peer(d) for d in range(1, n)]
     for where in peers:
@@ -149,9 +151,19 @@
         ref = tok_ref.at[s]
         return remote(ref, ref, tok_send.at[d - 1], tok_recv.at[d - 1], seq_peer(d))
 
-    start_halo(0)
     send_weight(0)
-    flag_ref[s] = jnp.broadcast_to(active_ref[...].astype(F32), flag_ref.shape[1:]).astype(BF16)
+    c_rows, wires = raw_ref.shape[0], raw_ref.shape[1]
+    blocks = raw_ref.shape[2] // 128
+    for b in range(blocks):
+        part = raw_ref[:, :, b * 128 : (b + 1) * 128].astype(F32)
+        split_ref[b] = part.reshape(c_rows * wires, 128)
+    for w in reversed(range(wires)):
+        cells = [split_ref[b, pl.ds(w, c_rows, stride=wires), :] for b in range(blocks)]
+        x_ref[w] = jnp.concatenate(cells, axis=1).astype(BF16)
+        if w == wires - 1:
+            start_halo(0)
+    copy_act.wait()
+    flag_ref[s] = jnp.broadcast_to(act_ref[...].astype(F32), flag_ref.shape[1:]).astype(BF16)
     for d in range(1, n):
         copy_flag(d).start()
 
@@ -220,12 +232,16 @@
     for d in range(1, n):
         copy_flag(d).wait_recv()
 
+    def order_column(k):
+        spread = jnp.broadcast_to(order_ref[pl.ds(k, 1), :].astype(F32), (count, count))
+        return jnp.transpose(spread)[:, 0:1].astype(jnp.int32)
+
     def activity(k, row):
-        block = order_ref[pl.ds(pl.multiple_of(k * count, count), count), :]
+        block = order_column(k)
         return row + dot(flag_ref[k], jnp.where(lanes == block, 1.0, 0.0).astype(BF16))
 
     row = lax.fori_loop(0, n, activity, jnp.zeros((flag_ref.shape[1], total_len), F32))
-    own = lanes == order_ref[pl.ds(pl.multiple_of(s * count, count), count), :]
+    own = lanes == order_column(s)
     onehot = jnp.where(own, 1.0, 0.0).astype(BF16)
     bias = jnp.where((row[0:1, :] > 0.5) | own, 0.0, -jnp.inf)
 
@@ -295,8 +311,8 @@
     readout, first_kernel, second_kernel, embed_weight, project_weight, output_weight, order, active
 ):
     n, n_mp, n_sec = lax.axis_size("seq"), lax.axis_size("mp"), lax.axis_size("section")
-    x = readout[0].transpose(1, 0, 2)
-    wires, c_in, ticks = x.shape
+    x = readout[0]
+    c_in, wires, ticks = x.shape
     c_mid, c_out = second_kernel.shape[2:]
     width = embed_weight.shape[1]
     rows_e = embed_weight.shape[0] // 4
@@ -311,7 +327,7 @@
     result = pl.pallas_call(
         functools.partial(kernel, (n, n_mp)),
         out_shape=jax.ShapeDtypeStruct((count, width), BF16),
-        in_specs=[vmem] * 5 + [hbm] * 3,
+        in_specs=[vmem] * 4 + [hbm] * 4,
         out_specs=vmem,
         scratch_shapes=[
             pltpu.VMEM((n_mp, n_sec, 4, rows_e, width), BF16),
@@ -328,6 +344,10 @@
             pltpu.VMEM((n, count, width), BF16),
             pltpu.VMEM((n * count, 2 * width), BF16),
             pltpu.VMEM((n, 16, count), BF16),
+            pltpu.VMEM((wires, c_in, ticks), BF16),
+            pltpu.VMEM((ticks // 128, c_in * wires, 128), F32),
+            pltpu.VMEM((1, count), jnp.int32),
+            dma,
             dma((4,)), dma((4,)), dma((4,)), dma(links), dma(links), dma(links), dma(links),
             dma(links + (2,)), dma(links + (2,)), dma((2,)), dma((2,)),
             dma((n - 1,)), dma((n - 1,)), dma((n - 1,)), dma((n - 1,)),
@@ -335,7 +355,7 @@
         compiler_params=pltpu.CompilerParams(
             collective_id=0, has_side_effects=True, vmem_limit_bytes=52 * 2**20
         ),
-    )(x, first_kernel, k2, order[0][:, None], active, embed, project_weight, output_weight)
+    )(x, first_kernel, k2, order.reshape(n, count), active, embed, project_weight, output_weight)
     return result[None]
 
 

time: 46.2 us -> 44.2 us (0.957)
  local copies, waits for them, and re-layouts: 4.86 us -> 2.86 us
    unnamed x14 -> x11, local copies, waits for them, and re-layouts: 3.58 us -> 1.69 us
where the time goes in v4:
time: 44.2 us; the launch traced here: 44 us
  Pallas kernels  41.1 us (93%)
  local copies, waits for them, and re-layouts  2.86 us (6%)
    pallas_call x1, Pallas kernels, body(): pl.pallas_call(functools.partial(kernel, (n, n_mp)), out_shape=jax.ShapeD...  41.1 us
    unnamed x11, local copies, waits for them, and re-layouts  1.69 us
    reshape x2, local copies, waits for them, and re-layouts, body(): embed = embed_weight.reshape(rows_e, 4, width).transpose(1, 0, 2)  1.18 us

profile of v4, /device:TPU:25, one launch (start us, length us, event | category | flops | bytes accessed | tf_op | source)
XLA Modules:
  0.0 44.0 jit_solution(13059895919001667537)
XLA Ops:
  0.0 0.0 copy-start.1
  0.0 1.1 %reshape.11 = bf16[64,4,768]{2,1,0:T(4,128)(2,1)S(1)} reshape(bf16[256,768]{1,0:T(8,128)(2,1)} %param.11) | data formatting | bytes 786432 | tf_op jit(solution)/shard_map/reshape | solution.py:319
  1.1 0.0 copy-start
  1.2 0.0 copy-start.2
  1.2 0.0 copy-start.3
  1.2 0.0 copy-start.4
  1.2 0.0 copy-done.1
  1.3 1.0 %copy-done = bf16[3,3,128,256]{3,2,1,0:T(8,128)(2,1)S(1)} copy-done((bf16[3,3,128,256]{3,2,1,0:T(8,128)(2,1)S(1)}, bf16[3,3,128,256]{3,2,1,0:T(8,128)(2,1)}, u32[]{:S(2)}) %copy-start) | copy-done | bytes 589848
  2.2 0.0 copy-done.2
  2.2 0.0 copy-done.3
  2.2 0.0 copy-done.4
  2.2 41.1 %shard_map.82 = bf16[128,768]{1,0:T(8,128)(2,1)S(1)} custom-call(bf16[64,8,1024]{2,1,0:T(8,128)(2,1)} %bitcast.11, bf16[3,3,64,128]{3,2,1,0:T(8,128)(2,1)S(1)} %copy-done.2, bf16[1152,256]{1,0:T(8,128)(2,1)S(1)} %bitcast.9, s32[4,128]{1,0:T(4,128)S(1)} %bitcast.10, s32[1,128]{1,0:T(1,128)S(1)} %copy-done.4, bf16[4,64,768]{2,1,0:T(8,128)(2,1)S(1)} %bitcast.7, ...), custom_call_target="tpu_custom_call" | custom-call | tf_op jit(solution)/shard_map/pallas_call | solution.py:327
  43.3 0.7 %copy.13 = bf16[1,128,768]{2,1,0:T(8,128)(2,1)} copy(bf16[1,128,768]{2,1,0:T(8,128)(2,1)S(1)} %bitcast.8) | data formatting | bytes 393216
  (1 shorter events, 0.0 us)
Async XLA Ops:
  0.0 1.2 %copy-start.1 = (bf16[192,768]{1,0:T(8,128)(2,1)S(1)}, bf16[192,768]{1,0:T(8,128)(2,1)}, u32[]{:S(2)}) copy-start(bf16[192,768]{1,0:T(8,128)(2,1)} %output_ref.1) | copy-start | bytes 884740
  1.1 1.1 %copy-start = (bf16[3,3,128,256]{3,2,1,0:T(8,128)(2,1)S(1)}, bf16[3,3,128,256]{3,2,1,0:T(8,128)(2,1)}, u32[]{:S(2)}) copy-start(bf16[3,3,128,256]{3,2,1,0:T(8,128)(2,1)} %param.10) | copy-start | bytes 1769476
  1.2 1.1 %copy-start.2 = (bf16[3,3,64,128]{3,2,1,0:T(8,128)(2,1)S(1)}, bf16[3,3,64,128]{3,2,1,0:T(8,128)(2,1)}, u32[]{:S(2)}) copy-start(bf16[3,3,64,128]{3,2,1,0:T(8,128)(2,1)} %k1_ref.1) | copy-start | bytes 442372
  1.2 1.1 %copy-start.3 = (s32[1,512]{1,0:T(1,128)S(1)}, s32[1,512]{1,0:T(1,128)}, u32[]{:S(2)}) copy-start(s32[1,512]{1,0:T(1,128)} %param.14) | copy-start | bytes 6148
  1.2 1.0 %copy-start.4 = (s32[1,128]{1,0:T(1,128)S(1)}, s32[1,128]{1,0:T(1,128)}, u32[]{:S(2)}) copy-start(s32[1,128]{1,0:T(1,128)} %active_ref.1) | copy-start | bytes 1540

commit v5 on v4

--- a/solution.py
+++ b/solution.py
@@ -260,7 +260,8 @@
     pass_y(2)
     pass_y(3)
 
-    def arrive(d, carry):
+    def arrive(step, carry):
+        d = lax.select(2 * s < n, n - step, step)
         copy_tok(d).wait_recv()
         place(lax.rem(s + n - d, n))
         return carry

time: 44.2 us -> 45.1 us (1.020)
  the two profiles are of different devices: /device:TPU:25 before, /device:TPU:9 now
where the time goes in v5:
time: 45.1 us; the launch traced here: 44.9 us
  Pallas kernels  42 us (93%)
  local copies, waits for them, and re-layouts  2.86 us (6%)
    pallas_call x1, Pallas kernels, body(): pl.pallas_call(functools.partial(kernel, (n, n_mp)), out_shape=jax.ShapeD...  42 us
    unnamed x11, local copies, waits for them, and re-layouts  1.69 us
    reshape x2, local copies, waits for them, and re-layouts, body(): embed = embed_weight.reshape(rows_e, 4, width).transpose(1, 0, 2)  1.18 us

profile of v5, /device:TPU:9, one launch (start us, length us, event | category | flops | bytes accessed | tf_op | source)
XLA Modules:
  0.0 44.9 jit_solution(3610154472438376643)
XLA Ops:
  0.0 0.0 copy-start.1
  0.0 1.1 %reshape.11 = bf16[64,4,768]{2,1,0:T(4,128)(2,1)S(1)} reshape(bf16[256,768]{1,0:T(8,128)(2,1)} %param.11) | data formatting | bytes 786432 | tf_op jit(solution)/shard_map/reshape | solution.py:320
  1.1 0.0 copy-start
  1.2 0.0 copy-start.2
  1.2 0.0 copy-start.3
  1.2 0.0 copy-start.4
  1.2 0.0 copy-done.1
  1.3 1.0 %copy-done = bf16[3,3,128,256]{3,2,1,0:T(8,128)(2,1)S(1)} copy-done((bf16[3,3,128,256]{3,2,1,0:T(8,128)(2,1)S(1)}, bf16[3,3,128,256]{3,2,1,0:T(8,128)(2,1)}, u32[]{:S(2)}) %copy-start) | copy-done | bytes 589848
  2.2 0.0 copy-done.2
  2.2 0.0 copy-done.3
  2.2 0.0 copy-done.4
  2.2 42.0 %shard_map.82 = bf16[128,768]{1,0:T(8,128)(2,1)S(1)} custom-call(bf16[64,8,1024]{2,1,0:T(8,128)(2,1)} %bitcast.11, bf16[3,3,64,128]{3,2,1,0:T(8,128)(2,1)S(1)} %copy-done.2, bf16[1152,256]{1,0:T(8,128)(2,1)S(1)} %bitcast.9, s32[4,128]{1,0:T(4,128)S(1)} %bitcast.10, s32[1,128]{1,0:T(1,128)S(1)} %copy-done.4, bf16[4,64,768]{2,1,0:T(8,128)(2,1)S(1)} %bitcast.7, ...), custom_call_target="tpu_custom_call" | custom-call | tf_op jit(solution)/shard_map/pallas_call | solution.py:328
  44.2 0.7 %copy.13 = bf16[1,128,768]{2,1,0:T(8,128)(2,1)} copy(bf16[1,128,768]{2,1,0:T(8,128)(2,1)S(1)} %bitcast.8) | data formatting | bytes 393216
  (1 shorter events, 0.0 us)
Async XLA Ops:
  0.0 1.2 %copy-start.1 = (bf16[192,768]{1,0:T(8,128)(2,1)S(1)}, bf16[192,768]{1,0:T(8,128)(2,1)}, u32[]{:S(2)}) copy-start(bf16[192,768]{1,0:T(8,128)(2,1)} %output_ref.1) | copy-start | bytes 884740
  1.1 1.1 %copy-start = (bf16[3,3,128,256]{3,2,1,0:T(8,128)(2,1)S(1)}, bf16[3,3,128,256]{3,2,1,0:T(8,128)(2,1)}, u32[]{:S(2)}) copy-start(bf16[3,3,128,256]{3,2,1,0:T(8,128)(2,1)} %param.10) | copy-start | bytes 1769476
  1.2 1.1 %copy-start.2 = (bf16[3,3,64,128]{3,2,1,0:T(8,128)(2,1)S(1)}, bf16[3,3,64,128]{3,2,1,0:T(8,128)(2,1)}, u32[]{:S(2)}) copy-start(bf16[3,3,64,128]{3,2,1,0:T(8,128)(2,1)} %k1_ref.1) | copy-start | bytes 442372
  1.2 1.1 %copy-start.3 = (s32[1,512]{1,0:T(1,128)S(1)}, s32[1,512]{1,0:T(1,128)}, u32[]{:S(2)}) copy-start(s32[1,512]{1,0:T(1,128)} %param.14) | copy-start | bytes 6148
  1.2 1.0 %copy-start.4 = (s32[1,128]{1,0:T(1,128)S(1)}, s32[1,128]{1,0:T(1,128)}, u32[]{:S(2)}) copy-start(s32[1,128]{1,0:T(1,128)} %active_ref.1) | copy-start | bytes 1540
